TPU v7x, 512 devices: a whole 4x8x8 slice. The times are simulated.
512 devices in a mesh: language: 8 (over y_hi, core), fsdp: 64 (over y_lo, x, z).
Axes of the slice: x: 4, y: 8 (y_hi: 4, y_lo: 2; y = y_hi * 2 + y_lo), z: 8, core: 2. Of those that a mesh axis runs over, the one named last changes fastest.
Arguments:
- hidden: bfloat16 [16, 8192, 5120], P('language', 'fsdp'), may hold values from -60 to 60
- latent_grad: bfloat16 [16, 8192, 64], P('language', 'fsdp'), may hold values from -0.15625 to 0.15625
- lang_ids: int32 [16], P('language'), may hold values from 0 to 15, each once
- old_weights: float32 [16], replicated, may hold values from 0.02 to 0.2
- param: float32 [5120, 64], P('fsdp'), may hold values from -6 to 6
- first_moment: float32 [5120, 64], P('fsdp'), may hold values from -6 to 6
- second_moment: float32 [5120, 64], P('fsdp'), may hold values from 0.25 to 4
Outputs:
- new_param: float32 [5120, 64], P('fsdp')
- new_first: float32 [5120, 64], P('fsdp')
- new_second: float32 [5120, 64], P('fsdp')
- new_logweights: float32 [16], replicated
Inputs may be any that keep to these rules, and one draw needn't show every extreme that they name: `lang_ids`: each id appears in exactly one slot.
All inputs are finite; a program needn't handle non-finite values.
Results may differ from a plain program's by a relative error of at most 0.0003.
Values may be sent and summed in bfloat16 or wider, within the bound.
A program may use at most 64 MiB of HBM per device.

v0:
```python
import jax
import jax.numpy as jnp
from jax import lax
from jax.sharding import PartitionSpec as P

STEP = 100


def log_weights(by_lang, square, old_weights):
    logits = jnp.log(old_weights) + old_weights.shape[0] * (by_lang / (square + 1e-06))
    return logits - jnp.log(jnp.sum(jnp.exp(logits)))


def local(hidden, latent_grad, lang_ids, old_weights, param, first_moment, second_moment):
    langs = old_weights.shape[0]
    slot_grad = lax.psum_scatter(
        jnp.einsum("ltd,ltr->dlr", hidden, latent_grad, preferred_element_type=jnp.float32),
        "fsdp",
        scatter_dimension=0,
        tiled=True,
    )
    onehot = (lang_ids[:, None] == jnp.arange(langs, dtype=jnp.int32)[None, :]).astype(jnp.float32)
    total = lax.psum(jnp.sum(slot_grad, axis=1), "language")
    dots = jnp.einsum("dlr,dr->l", slot_grad, total, precision=lax.Precision.HIGHEST)
    leader = (lax.axis_index("language") == 0).astype(jnp.float32)
    square_part = jnp.sum(total * total) * leader
    by_lang_part = jnp.dot(dots, onehot, precision=lax.Precision.HIGHEST)
    by_lang, square = lax.psum((by_lang_part, square_part), ("language", "fsdp"))
    new_logweights = log_weights(by_lang, square, old_weights)
    weights = jnp.exp(new_logweights)
    slot_weight = jnp.dot(onehot, weights, precision=lax.Precision.HIGHEST)
    local_update = jnp.einsum("l,dlr->dr", slot_weight, slot_grad, precision=lax.Precision.HIGHEST)
    update = lax.psum(local_update, "language")
    new_first = 0.9 * first_moment + 0.1 * update
    new_second = 0.95 * second_moment + 0.05 * update * update
    first_hat = new_first / (1.0 - 0.9**STEP)
    second_hat = new_second / (1.0 - 0.95**STEP)
    new_param = param - 0.02 * (first_hat / (jnp.sqrt(second_hat) + 1e-08) + 0.1 * param)
    return (new_param, new_first, new_second, new_logweights)


def solution(mesh):
    placed = (
        P("language", "fsdp", None),
        P("language", "fsdp", None),
        P("language"),
        P(),
        P("fsdp", None),
        P("fsdp", None),
        P("fsdp", None),
    )
    return jax.shard_map(
        local,
        mesh=mesh,
        in_specs=placed,
        out_specs=(P("fsdp", None), P("fsdp", None), P("fsdp", None), P()),
        check_vma=False,
    )
```

profile of v0, /device:TPU:2, one launch (start us, length us, event | category | flops | bytes accessed | tf_op | source)
XLA Modules:
  0.0 505.8 jit_solution(7632736756905314304)
XLA Ops:
  7.2 0.0 copy-start
  7.2 0.0 reduce-scatter.4.cloned.1.call-start
  7.2 1.7 copy-done
  8.9 2.8 fusion.7
  11.7 3.2 copy.16
  14.9 0.0 copy-start.5
  14.9 0.0 copy-start.4
  14.9 0.0 copy-start.1
  14.9 0.0 copy-start.2
  14.9 0.0 copy-start.3
  14.9 0.0 reduce-scatter.4.cloned.1.call-update
  15.0 310.9 %reduce-scatter.4.cloned.1.call-done = f32[80,128]{1,0:T(8,128)} async-done(((f32[5120,128]{1,0:T(8,128)}), f32[80,128]{1,0:T(8,128)}) %reduce-scatter.4.cloned.1.call-update) | async-done | bytes 40976
  325.9 0.9 copy.17
  326.8 27.2 %psum.28 = f32[80,64]{0,1:T(8,128)S(1)} all-reduce(f32[80,64]{0,1:T(8,128)S(1)} %reduce_sum.27), channel_id=1, replica_groups=mesh['language'=8,'fsdp'=64] {'language'}, use_global_device_ids=true, to_apply=%region_2.0 | all-reduce | flops 5120 | bytes 40960 | tf_op jit(solution)/shard_map/psum | solution.py:23
  354.0 0.6 multiply_reduce_fusion
  354.6 0.7 convolution_bitcast_fusion.2
  355.3 0.0 copy-done.5
  355.3 0.2 convolution_bitcast_fusion.1
  356.1 111.2 %all-reduce = (f32[16]{0:T(128)S(1)}, f32[]{:T(128)}) all-reduce(f32[16]{0:T(128)S(1)} %convolution_bitcast_fusion.1, f32[]{:T(128)S(6)} %mul.45), channel_id=1, replica_groups=mesh['language'=8,'fsdp'=64] {'language','fsdp'}, use_global_device_ids=true, to_apply=%region_3.0 | all-reduce | flops 17 | bytes 136 | tf_op jit(solution)/shard_map/psum | solution.py:28
  468.0 0.0 copy-done.4
  468.0 0.6 exponential_reduce_fusion
  469.3 0.0 copy-start.6
  469.3 0.2 convolution_bitcast_fusion
  469.5 0.4 fusion
  469.9 28.4 %psum.31 = f32[80,64]{0,1:T(8,128)S(1)} all-reduce(f32[80,64]{0,1:T(8,128)S(1)} %bitcast.34), channel_id=1, replica_groups=mesh['language'=8,'fsdp'=64] {'language'}, use_global_device_ids=true, to_apply=%region_7.0 | all-reduce | flops 5120 | bytes 40960 | tf_op jit(solution)/shard_map/psum | solution.py:33
  498.3 0.0 copy-done.1
  498.3 0.0 copy-done.2
  498.3 0.0 copy-done.3
  498.3 0.7 multiply_subtract_fusion
  499.0 0.0 copy-done.6
  (2 shorter events, 0.0 us)
Async XLA Ops:
  7.2 1.7 copy-start
  7.2 318.7 %reduce-scatter.4.cloned.1.call-start = ((), (), s32[]{:S(2)}) async-start(), calls=%async_computation.1 | async-start | bytes 2662400
  14.9 340.3 %copy-start.5 = (s32[2]{0:T(128)S(1)}, s32[2]{0:T(128)}, u32[]{:S(2)}) copy-start(s32[2]{0:T(128)} %param.9) | copy-start | bytes 28
  14.9 453.1 %copy-start.4 = (f32[16]{0:T(128)S(1)}, f32[16]{0:T(128)}, u32[]{:S(2)}) copy-start(f32[16]{0:T(128)} %param.10) | copy-start | bytes 196
  14.9 483.4 %copy-start.1 = (f32[80,64]{0,1:T(8,128)S(1)}, f32[80,64]{0,1:T(8,128)}, u32[]{:S(2)}) copy-start(f32[80,64]{0,1:T(8,128)} %param.11) | copy-start | bytes 61444
  14.9 483.4 %copy-start.2 = (f32[80,64]{0,1:T(8,128)S(1)}, f32[80,64]{0,1:T(8,128)}, u32[]{:S(2)}) copy-start(f32[80,64]{0,1:T(8,128)} %param.12) | copy-start | bytes 61444
  14.9 483.4 %copy-start.3 = (f32[80,64]{0,1:T(8,128)S(1)}, f32[80,64]{0,1:T(8,128)}, u32[]{:S(2)}) copy-start(f32[80,64]{0,1:T(8,128)} %param.13) | copy-start | bytes 61444
  469.3 29.7 %copy-start.6 = (f32[16]{0:T(128)}, f32[16]{0:T(128)S(1)}, u32[]{:S(2)}) copy-start(f32[16]{0:T(128)S(1)} %broadcast_subtract_fusion) | copy-start | bytes 196
Sparse Core Ops, SparseCore 0:
  15.1 310.7 reduce-scatter.3
where the time goes:
time: 506 us
  waiting for transfers between devices  311 us (61%)
  blocking collectives  167 us (33%)
  between operations  16.1 us (3%)
  local copies, waits for them, and re-layouts  5.81 us (1%)
    unnamed x2, waiting for transfers between devices  311 us
    psum x1, blocking collectives, local(): lax.psum((by_lang_part, square_part), ('language', 'fsdp'))  111 us
    psum x1, blocking collectives, local(): update = lax.psum(local_update, 'language')  28.4 us
    psum x1, blocking collectives, local(): total = lax.psum(jnp.sum(slot_grad, axis=1), 'language')  27.2 us
  transfers between devices with their start and end apart: 1, of which 1 were waited for; matrix products, arithmetic and copies ran while one was open for 0% of the time, Pallas kernels for 0%

commit v1 on v0

--- a/solution.py
+++ b/solution.py
@@ -25,7 +25,7 @@
     leader = (lax.axis_index("language") == 0).astype(jnp.float32)
     square_part = jnp.sum(total * total) * leader
     by_lang_part = jnp.dot(dots, onehot, precision=lax.Precision.HIGHEST)
-    by_lang, square = lax.psum((by_lang_part, square_part), ("language", "fsdp"))
+    by_lang, square = lax.psum(lax.psum((by_lang_part, square_part), "language"), "fsdp")
     new_logweights = log_weights(by_lang, square, old_weights)
     weights = jnp.exp(new_logweights)
     slot_weight = jnp.dot(onehot, weights, precision=lax.Precision.HIGHEST)

time: 506 us -> 578 us (1.14)
  the two profiles are of different devices: /device:TPU:2 before, /device:TPU:40 now
where the time goes in v1:
time: 578 us
  waiting for transfers between devices  327 us (57%)
  blocking collectives  223 us (39%)
  between operations  16.1 us (3%)
  local copies, waits for them, and re-layouts  5.81 us (1%)
    unnamed x2, waiting for transfers between devices  327 us
    psum x1, blocking collectives, local(): lax.psum(lax.psum((by_lang_part, square_part), 'language'), 'fsdp')  154 us
    psum x1, blocking collectives, local(): update = lax.psum(local_update, 'language')  27.2 us
    psum x1, blocking collectives, local(): total = lax.psum(jnp.sum(slot_grad, axis=1), 'language')  27.2 us
    psum x1, blocking collectives, local(): lax.psum((by_lang_part, square_part), 'language')  14.7 us
  transfers between devices with their start and end apart: 1, of which 1 were waited for; matrix products, arithmetic and copies ran while one was open for 0% of the time, Pallas kernels for 0%

profile of v1, /device:TPU:40, one launch (start us, length us, event | category | flops | bytes accessed | tf_op | source)
XLA Modules:
  0.0 577.8 jit_solution(12708192756847903330)
XLA Ops:
  7.2 0.0 copy-start
  7.2 0.0 reduce-scatter.4.cloned.1.call-start
  7.2 1.7 copy-done
  8.9 2.8 fusion.7
  11.7 3.2 copy.16
  14.9 0.0 copy-start.5
  14.9 0.0 copy-start.4
  14.9 0.0 copy-start.1
  14.9 0.0 copy-start.2
  14.9 0.0 copy-start.3
  14.9 0.0 reduce-scatter.4.cloned.1.call-update
  15.0 326.5 %reduce-scatter.4.cloned.1.call-done = f32[80,128]{1,0:T(8,128)} async-done(((f32[5120,128]{1,0:T(8,128)}), f32[80,128]{1,0:T(8,128)}) %reduce-scatter.4.cloned.1.call-update) | async-done | bytes 40976
  341.5 0.9 copy.17
  342.4 27.2 %psum.42 = f32[80,64]{0,1:T(8,128)S(1)} all-reduce(f32[80,64]{0,1:T(8,128)S(1)} %reduce_sum.27), channel_id=1, replica_groups=mesh['language'=8,'fsdp'=64] {'language'}, use_global_device_ids=true, to_apply=%region_2.0 | all-reduce | flops 5120 | bytes 40960 | tf_op jit(solution)/shard_map/psum | solution.py:23
  369.6 0.6 multiply_reduce_fusion
  370.2 0.7 convolution_bitcast_fusion.2
  370.9 0.0 copy-done.5
  370.9 0.2 convolution_bitcast_fusion.1
  371.7 14.7 %all-reduce.1 = (f32[16]{0:T(128)S(1)}, f32[]{:T(128)}) all-reduce(f32[16]{0:T(128)S(1)} %convolution_bitcast_fusion.1, f32[]{:T(128)S(6)} %mul.45), channel_id=1, replica_groups=mesh['language'=8,'fsdp'=64] {'language'}, use_global_device_ids=true, to_apply=%region_3.0 | all-reduce | flops 17 | bytes 136 | tf_op jit(solution)/shard_map/psum | solution.py:28
  386.5 154.1 %all-reduce = (f32[16]{0:T(128)S(1)}, f32[]{:T(128)}) all-reduce(f32[16]{0:T(128)S(1)} %get-tuple-element.6, f32[]{:T(128)} %get-tuple-element.7), channel_id=1, replica_groups=mesh['language'=8,'fsdp'=64] {'fsdp'}, use_global_device_ids=true, to_apply=%region_4.0 | all-reduce | flops 17 | bytes 136 | tf_op jit(solution)/shard_map/psum | solution.py:28
  541.2 0.0 copy-done.4
  541.2 0.6 exponential_reduce_fusion
  542.5 0.0 copy-start.6
  542.5 0.2 convolution_bitcast_fusion
  542.7 0.4 fusion
  543.1 27.2 %psum.47 = f32[80,64]{0,1:T(8,128)S(1)} all-reduce(f32[80,64]{0,1:T(8,128)S(1)} %bitcast.34), channel_id=1, replica_groups=mesh['language'=8,'fsdp'=64] {'language'}, use_global_device_ids=true, to_apply=%region_9.0 | all-reduce | flops 5120 | bytes 40960 | tf_op jit(solution)/shard_map/psum | solution.py:33
  570.3 0.0 copy-done.1
  570.3 0.0 copy-done.2
  570.3 0.0 copy-done.3
  570.3 0.7 multiply_subtract_fusion
  571.0 0.0 copy-done.6
  (2 shorter events, 0.0 us)
Async XLA Ops:
  7.2 1.7 copy-start
  7.2 334.3 %reduce-scatter.4.cloned.1.call-start = ((), (), s32[]{:S(2)}) async-start(), calls=%async_computation.1 | async-start | bytes 2662400
  14.9 356.0 %copy-start.5 = (s32[2]{0:T(128)S(1)}, s32[2]{0:T(128)}, u32[]{:S(2)}) copy-start(s32[2]{0:T(128)} %param.9) | copy-start | bytes 28
  14.9 526.3 %copy-start.4 = (f32[16]{0:T(128)S(1)}, f32[16]{0:T(128)}, u32[]{:S(2)}) copy-start(f32[16]{0:T(128)} %param.10) | copy-start | bytes 196
  14.9 555.4 %copy-start.1 = (f32[80,64]{0,1:T(8,128)S(1)}, f32[80,64]{0,1:T(8,128)}, u32[]{:S(2)}) copy-start(f32[80,64]{0,1:T(8,128)} %param.11) | copy-start | bytes 61444
  14.9 555.4 %copy-start.2 = (f32[80,64]{0,1:T(8,128)S(1)}, f32[80,64]{0,1:T(8,128)}, u32[]{:S(2)}) copy-start(f32[80,64]{0,1:T(8,128)} %param.12) | copy-start | bytes 61444
  14.9 555.3 %copy-start.3 = (f32[80,64]{0,1:T(8,128)S(1)}, f32[80,64]{0,1:T(8,128)}, u32[]{:S(2)}) copy-start(f32[80,64]{0,1:T(8,128)} %param.13) | copy-start | bytes 61444
  542.5 28.4 %copy-start.6 = (f32[16]{0:T(128)}, f32[16]{0:T(128)S(1)}, u32[]{:S(2)}) copy-start(f32[16]{0:T(128)S(1)} %broadcast_subtract_fusion) | copy-start | bytes 196
Sparse Core Ops, SparseCore 0:
  15.1 326.3 reduce-scatter.3
